TPU v7x, 512 devices: a whole 4x4x16 slice. The times are simulated.
512 devices in a mesh: row: 16 (over x, y_lo, core), chan: 32 (over z, y_hi).
Axes of the slice: x: 4, y: 4 (y_hi: 2, y_lo: 2; y = y_hi * 2 + y_lo), z: 16, core: 2. Of those that a mesh axis runs over, the one named last changes fastest.
Arguments:
- pair: bfloat16 [1280, 1280, 128], P('row', 'chan'), may hold values from -6 to 6
- w_left_gate: bfloat16 [128, 128], replicated, may hold values from -0.5 to 0.5
- w_left: bfloat16 [128, 128], replicated, may hold values from -0.5 to 0.5
- w_right_gate: bfloat16 [128, 128], replicated, may hold values from -0.5 to 0.5
- w_right: bfloat16 [128, 128], replicated, may hold values from -0.5 to 0.5
- w_out_gate: bfloat16 [128, 128], replicated, may hold values from -0.5 to 0.5
- w_out: bfloat16 [128, 128], replicated, may hold values from -0.5 to 0.5
Outputs:
- update: bfloat16 [1280, 1280, 128], P('row', 'chan')
All inputs are finite; a program needn't handle non-finite values.
Results may differ from a plain program's by a relative error of at most 0.0083.
Values may be sent and summed in bfloat16 or wider, within the bound.
A program may use at most 64 MiB of HBM per device.

v0:
```python
import jax
import jax.numpy as jnp
from jax import lax
from jax.sharding import PartitionSpec as P


def layer_norm(values, axis):
    mean = jnp.mean(values, axis=axis, keepdims=True)
    centered = values - mean
    variance = jnp.mean(centered * centered, axis=axis, keepdims=True)
    return centered * lax.rsqrt(variance + 1e-05)


def on_device(pair, w_left_gate, w_left, w_right_gate, w_right, w_out_gate, w_out):
    row_count, col_count, channels = pair.shape
    hidden = w_left.shape[1]
    normed = layer_norm(pair.astype(jnp.float32), -1).astype(jnp.bfloat16)
    flat = normed.reshape(row_count * col_count, channels)

    def factor(weight_gate, weight_proj):
        gate_value = jnp.einsum("pc,ch->hp", flat, weight_gate, preferred_element_type=jnp.float32)
        proj_value = jnp.einsum("pc,ch->hp", flat, weight_proj, preferred_element_type=jnp.float32)
        joined = (jax.nn.sigmoid(gate_value) * proj_value).astype(jnp.bfloat16)
        return joined.reshape(hidden, row_count, col_count)

    left_local = factor(w_left_gate, w_left)
    right_local = factor(w_right_gate, w_right)
    left_slab, right_slab = (
        lax.all_to_all(left_local, "chan", split_axis=0, concat_axis=2, tiled=True),
        lax.all_to_all(right_local, "chan", split_axis=0, concat_axis=2, tiled=True),
    )
    right_all = lax.all_gather(right_slab, "row", axis=1, tiled=True)
    combined_wide = jnp.einsum(
        "hik,hjk->hij", left_slab, right_all, preferred_element_type=jnp.float32
    )
    combined_slab = combined_wide.astype(jnp.bfloat16)
    combined = lax.all_to_all(combined_slab, "chan", split_axis=2, concat_axis=0, tiled=True)
    combined_normed = layer_norm(combined.astype(jnp.float32), 0).astype(jnp.bfloat16)
    combined_flat = combined_normed.reshape(hidden, row_count * col_count)
    linear = jnp.einsum("hp,hc->pc", combined_flat, w_out, preferred_element_type=jnp.float32)
    gate = jax.nn.sigmoid(jnp.dot(flat, w_out_gate, preferred_element_type=jnp.float32))
    return (gate * linear).astype(jnp.bfloat16).reshape(row_count, col_count, channels)


def solution(mesh):
    in_specs = (P("row", "chan", None), P(), P(), P(), P(), P(), P())
    out_specs = P("row", "chan", None)
    return jax.shard_map(
        on_device, mesh=mesh, in_specs=in_specs, out_specs=out_specs, check_vma=False
    )
```

profile of v0, /device:TPU:1, one launch (start us, length us, event | category | flops | bytes accessed | tf_op | source)
XLA Modules:
  0.0 300.5 jit_solution(5436306838506156358)
XLA Ops:
  6.5 0.0 copy-start
  6.5 0.0 copy-start.1
  6.5 0.0 all-gather.2.cloned.1.call-start
  6.5 1.7 convert_reduce_fusion
  8.3 2.1 fusion.14
  10.4 0.0 copy-done.1
  10.4 1.0 fusion.15
  11.4 0.0 copy-done
  11.4 0.0 copy-start.2
  11.4 0.6 fusion.2
  12.0 0.2 copy-done.2
  12.2 0.3 fusion.10
  12.6 1.4 copy.34
  14.0 83.7 %all_to_all.45 = bf16[128,80,40]{1,2,0:T(8,128)(2,1)S(1)} all-to-all(bf16[128,80,40]{1,2,0:T(8,128)(2,1)S(1)} %copy.34), channel_id=1, replica_groups=mesh['row'=16,'chan'=32] {'chan'}, dimensions={0} | all-to-all | bytes 1638400 | tf_op jit(solution)/shard_map/all_to_all | solution.py:30
  97.7 0.1 copy.35
  97.8 0.0 copy-start.5
  97.8 1.3 copy.36
  99.2 0.0 all-gather.2.cloned.1.call-update
  99.2 0.0 copy-done.5
  99.2 0.0 copy-start.3
  99.2 0.6 fusion.5
  99.8 0.2 copy-done.3
  100.0 0.4 fusion.9
  100.3 1.4 copy.32
  101.7 70.6 %all_to_all.46 = bf16[128,80,40]{1,2,0:T(8,128)(2,1)S(1)} all-to-all(bf16[128,80,40]{1,2,0:T(8,128)(2,1)S(1)} %copy.32), channel_id=1, replica_groups=mesh['row'=16,'chan'=32] {'chan'}, dimensions={0} | all-to-all | bytes 1638400 | tf_op jit(solution)/shard_map/all_to_all | solution.py:29
  172.3 0.1 copy.33
  172.4 15.3 %all-gather.2.cloned.1.call-done = bf16[4,1280,1280]{2,1,0:T(8,128)(2,1)} async-done(((bf16[4,80,1280]{2,1,0:T(8,128)(2,1)}), bf16[4,1280,1280]{2,1,0:T(8,128)(2,1)}) %all-gather.2.cloned.1.call-update) | async-done | bytes 13107216 | tf_op jit(solution)/shard_map/all_gather | solution.py:32
  187.7 8.8 %convolution_convert_fusion = bf16[4,80,1280]{2,1,0:T(8,128)(2,1)S(1)} fusion(bf16[4,80,1280]{1,2,0:T(8,128)(2,1)S(1)} %bitcast.50, bf16[4,1280,1280]{2,1,0:T(8,128)(2,1)} %all-gather.2.cloned.1.call-done), kind=kOutput, calls=%fused_computation.18 | convolution fusion | flops 1048985600 | bytes 14745600 | tf_op jit(solution)/shard_map/hik,hjk->hij/dot_general | solution.py:33
  196.5 2.2 copy.38
  198.6 0.0 copy-start.6
  198.6 14.8 %all-to-all-start.2 = ((bf16[4,80,1280]{1,0,2:T(4,128)(2,1)}), bf16[4,80,1280]{1,0,2:T(4,128)(2,1)S(1)}, u32[]{:S(2)}, u32[]{:S(2)}) async-start(bf16[4,80,1280]{1,0,2:T(4,128)(2,1)} %copy.38), calls=%async_computation.2 | async-start | bytes 2621440 | tf_op jit(solution)/shard_map/all_to_all | solution.py:37
  213.5 0.0 copy-done.6
  213.5 1.8 fusion.8
  215.3 62.6 %all-to-all-done.2 = bf16[4,80,1280]{1,0,2:T(4,128)(2,1)S(1)} async-done(((bf16[4,80,1280]{1,0,2:T(4,128)(2,1)}), bf16[4,80,1280]{1,0,2:T(4,128)(2,1)S(1)}, u32[]{:S(2)}, u32[]{:S(2)}) %all-to-all-start.2) | async-done | bytes 819232 | tf_op jit(solution)/shard_map/all_to_all | solution.py:37
  277.9 0.2 copy.39
  278.0 0.3 fusion.16
  278.3 0.1 copy.41
  278.4 0.1 div.37
  278.5 0.1 copy.42
  278.6 1.7 convert_bitcast_fusion
  280.3 0.5 multiply_reduce_fusion
  280.7 0.1 copy.43
  280.9 0.1 rsqrt.21
  280.9 5.2 %copy.40 = f32[32,4,80,40]{3,2,1,0:T(8,128)} copy(f32[32,4,80,40]{2,3,0,1:T(8,128)} %convert_bitcast_fusion) | data formatting | bytes 3276800 | tf_op jit(solution)/shard_map/convert_element_type | solution.py:38
  286.2 0.0 copy-start.4
  286.2 4.7 %reshape.61 = f32[128,3200]{1,0:T(8,128)S(1)} reshape(f32[32,4,80,40]{3,2,1,0:T(8,128)} %copy.40) | data formatting | bytes 3276800 | tf_op jit(solution)/shard_map/convert_element_type | solution.py:38
  290.9 0.0 copy-done.4
  290.9 2.7 fusion.11
  (4 shorter events, 0.0 us)
Async XLA Ops:
  6.5 4.9 %copy-start = (bf16[128,128]{1,0:T(8,128)(2,1)S(1)}, bf16[128,128]{1,0:T(8,128)(2,1)}, u32[]{:S(2)}) copy-start(bf16[128,128]{1,0:T(8,128)(2,1)} %param.10) | copy-start | bytes 98308
  6.5 3.8 %copy-start.1 = (bf16[80,40,128]{2,1,0:T(8,128)(2,1)S(1)}, bf16[80,40,128]{2,1,0:T(8,128)(2,1)}, u32[]{:S(2)}) copy-start(bf16[80,40,128]{2,1,0:T(8,128)(2,1)} %param.7) | copy-start | bytes 2457604
  6.5 181.1 %all-gather.2.cloned.1.call-start = ((), (), s32[]{:S(2)}) async-start(), calls=%async_computation.3 | async-start | bytes 13926400 | tf_op jit(solution)/shard_map/all_gather | solution.py:32
  11.4 0.8 copy-start.2
  97.8 1.4 copy-start.5
  99.2 0.8 copy-start.3
  198.6 14.8 %copy-start.6 = (bf16[128,128]{1,0:T(8,128)(2,1)S(1)}, bf16[128,128]{1,0:T(8,128)(2,1)}, u32[]{:S(2)}) copy-start(bf16[128,128]{1,0:T(8,128)(2,1)} %param.12) | copy-start | bytes 98308
  198.6 79.2 %all-to-all-start.2 = ((bf16[4,80,1280]{1,0,2:T(4,128)(2,1)}), bf16[4,80,1280]{1,0,2:T(4,128)(2,1)S(1)}, u32[]{:S(2)}, u32[]{:S(2)}) async-start(bf16[4,80,1280]{1,0,2:T(4,128)(2,1)} %copy.38), calls=%async_computation.2 | async-start | bytes 2621440 | tf_op jit(solution)/shard_map/all_to_all | solution.py:37
  286.2 4.7 %copy-start.4 = (bf16[128,128]{1,0:T(8,128)(2,1)S(1)}, bf16[128,128]{1,0:T(8,128)(2,1)}, u32[]{:S(2)}) copy-start(bf16[128,128]{1,0:T(8,128)(2,1)} %param.13) | copy-start | bytes 98308
Sparse Core Ops, SparseCore 0:
  99.3 88.3 all-gather.1
where the time goes:
time: 301 us; the launch traced here: 300 us
  blocking collectives  154 us (51%)
  waiting for transfers between devices  77.8 us (26%)
  local copies, waits for them, and re-layouts  17.4 us (6%)
  matrix products  15.2 us (5%)
  starting transfers between devices  14.8 us (5%)
  between operations  13.6 us (5%)
  other arithmetic  7.33 us (2%)
    all_to_all x1, blocking collectives, on_device(): lax.all_to_all(right_local, 'chan', split_axis=0, concat_axis=2, tiled=True)  83.7 us
    all_to_all x1, blocking collectives, on_device(): lax.all_to_all(left_local, 'chan', split_axis=0, concat_axis=2, tiled=True)  70.6 us
    all_to_all x1, waiting for transfers between devices, on_device(): lax.all_to_all(combined_slab, 'chan', split_axis=2, concat_axis=0, tiled=...  62.6 us
    all_gather x1, waiting for transfers between devices, on_device(): right_all = lax.all_gather(right_slab, 'row', axis=1, tiled=True)  15.3 us
    all_to_all x1, starting transfers between devices, on_device(): lax.all_to_all(combined_slab, 'chan', split_axis=2, concat_axis=0, tiled=...  14.8 us
    convert_element_type x2, local copies, waits for them, and re-layouts, on_device(): combined.astype(jnp.float32)  9.9 us
    dot_general x1, matrix products, on_device(): jnp.einsum('hik,hjk->hij', left_slab, right_all, preferred_element_type=j...  8.81 us
  transfers between devices with their start and end apart: 2, of which 2 were waited for; matrix products, arithmetic and copies ran while one was open for 1% of the time, Pallas kernels for 0%

commit v1 on v0

v1 whole, which is shorter than its diff:
```python
import functools

import jax
import jax.numpy as jnp
from jax import lax
from jax.experimental import pallas as pl
from jax.experimental.pallas import tpu as pltpu
from jax.sharding import PartitionSpec as P

MESH = pl.DeviceIdType.MESH
F32, BF16 = jnp.float32, jnp.bfloat16
EPS = 1e-05
ROWS, COLS, CH = 80, 40, 128
PLANES, CHUNKS, STEP = 16, 5, 8
WIDE = STEP * ROWS
SHORT, SHORT_PAD = WIDE // 2, 384


def nt(a, b):
    return lax.dot_general(a, b, (((1,), (1,)), ((), ())), preferred_element_type=F32)


def tn(a, b):
    return lax.dot_general(a, b, (((0,), (0,)), ((), ())), preferred_element_type=F32)


def unfold(x, k):
    start = k * ROWS
    tile, off = start // 128, start % 128
    lo = x[:, tile * 128 : tile * 128 + 128]
    if off == 0:
        return lo
    lo = pltpu.roll(lo, 128 - off, 1)
    if off + ROWS <= 128:
        return lo
    hi = pltpu.roll(x[:, tile * 128 + 128 : tile * 128 + 256], 128 - off, 1)
    lane = lax.broadcasted_iota(jnp.int32, lo.shape, 1)
    return jnp.where(lane < 128 - off, lo, hi)


def fold(pieces):
    tiles = [None] * (-(-len(pieces) * ROWS // 128))
    lane = lax.broadcasted_iota(jnp.int32, pieces[0].shape, 1)
    for k, piece in enumerate(pieces):
        start = k * ROWS
        tile, off = start // 128, start % 128
        turned = pltpu.roll(piece, off, 1) if off else piece
        tiles[tile] = turned if tiles[tile] is None else jnp.where(lane < off, tiles[tile], turned)
        if off + ROWS > 128:
            tiles[tile + 1] = turned
    return jnp.concatenate(tiles, axis=1)


def kernel(
    pair_ref, wlg_ref, wl_ref, wrg_ref, wr_ref, wog_ref, wo_ref, out_ref,
    pair32, wt, ns, normed, gate, send, got, unf, tiles, left, right, acc, osend, oback, fbuf, fold_send, fold_got, lin,
    zs, zr, pls, prs, plr, prr, os_, or_, fs, fr,
):
    r, c = lax.axis_index("row"), lax.axis_index("chan")
    z, y = c // 2, lax.rem(c, 2)
    a, t, b = r // 8, lax.rem(r, 8), lax.rem(r, 2)
    h = (t // 2) * 2 + y
    half = pl.multiple_of(y * 128, 128)

    def owner(h_, a_, b_):
        return (a_ * 8 + (h_ // 2) * 2 + b_, z * 2 + lax.rem(h_, 2))

    def at_plane(z_):
        return (r, z_ * 2 + y)

    barrier = pltpu.get_barrier_semaphore()

    def greet_plane(d, carry):
        pl.semaphore_signal(barrier, inc=1, device_id=at_plane(lax.rem(z + d, PLANES)), device_id_type=MESH)
        return carry

    def greet_inside(d, carry):
        there = (lax.rem(r + d // 2, 16), z * 2 + lax.rem(y + lax.rem(d, 2), 2))
        pl.semaphore_signal(barrier, inc=1, device_id=there, device_id_type=MESH)
        return carry

    lax.fori_loop(1, PLANES, greet_plane, 0)
    lax.fori_loop(1, 32, greet_inside, 0)

    for n, ref in enumerate((wlg_ref, wl_ref, wrg_ref, wr_ref)):
        wt[n] = ref[...].astype(F32).T.astype(BF16)
    pair32[...] = pair_ref[...].astype(F32)

    def normalise(s):
        def eight_rows(g, carry):
            x = pair32[pl.ds(pl.multiple_of(g * 8, 8), 8), pl.ds(pl.multiple_of(s * STEP, STEP), STEP), :]
            centered = x - jnp.mean(x, axis=-1, keepdims=True)
            variance = jnp.mean(centered * centered, axis=-1, keepdims=True)
            at = pl.multiple_of(lax.rem(g, 5) * 16 + (g // 5) * 8, 8)
            ns[:, pl.ds(at, 8), :] = jnp.swapaxes(centered * lax.rsqrt(variance + EPS), 0, 1)
            return carry

        lax.fori_loop(0, 10, eight_rows, 0)
        normed[s] = ns[...].reshape(WIDE, CH).astype(BF16)

    def factors(s):
        n = normed[s]
        lf = (jax.nn.sigmoid(nt(wt[0], n)) * nt(wt[1], n)).reshape(PLANES, 8, WIDE)
        rf = (jax.nn.sigmoid(nt(wt[2], n)) * nt(wt[3], n)).reshape(PLANES, 8, WIDE)
        send[s] = jnp.concatenate([lf, rf], axis=1).astype(BF16)

    def send_planes(s):
        pltpu.make_async_copy(send.at[s, z], got.at[s, z], zr.at[s]).start()

        def one(d, carry):
            there = lax.rem(z + d, PLANES)
            pltpu.make_async_remote_copy(
                src_ref=send.at[s, there], dst_ref=got.at[s, z], send_sem=zs.at[s], recv_sem=zr.at[s],
                device_id=at_plane(there), device_id_type=MESH,
            ).start()
            return carry

        lax.fori_loop(1, PLANES, one, 0)

    def unfold_chunk(s):
        def two_planes(m, carry):
            for e in range(2):
                x = got[s, 2 * m + e].astype(F32)
                for k in range(STEP):
                    unf[:, e * STEP + k, :] = unfold(x, k)
            tiles[s, :, pl.ds(pl.multiple_of(m * 16, 16), 16), :] = unf[...].astype(BF16)
            return carry

        lax.fori_loop(0, PLANES // 2, two_planes, 0)

    def send_inside(s):
        to_left = left.at[s, pl.ds(half, 128), pl.ds(pl.multiple_of(t * 128, 128), 128)]
        to_right = right.at[s, pl.ds(half, 128), pl.ds(pl.multiple_of((r // 2) * 128, 128), 128)]
        for e in range(2):

            def one(d, carry, e=e):
                there = lax.rem(h + d, 8)
                pltpu.make_async_remote_copy(
                    src_ref=tiles.at[s, there], dst_ref=to_left, send_sem=pls.at[s], recv_sem=plr.at[s],
                    device_id=owner(there, a, lax.rem(b + e, 2)), device_id_type=MESH,
                ).start()
                pltpu.make_async_remote_copy(
                    src_ref=tiles.at[s, 8 + there], dst_ref=to_right, send_sem=prs.at[s], recv_sem=prr.at[s],
                    device_id=owner(there, lax.rem(a + e, 2), b), device_id_type=MESH,
                ).start()
                return carry

            lax.fori_loop(1 - e, 8, one, 0)
        pltpu.make_async_copy(tiles.at[s, h], to_left, plr.at[s]).start()
        pltpu.make_async_copy(tiles.at[s, 8 + h], to_right, prr.at[s]).start()

    def multiply(s, first):
        pltpu.make_async_copy(left.at[s], left.at[s], plr.at[s]).wait()
        pltpu.make_async_copy(right.at[s], right.at[s], prr.at[s]).wait()

        def one(m, carry):
            cols = right[s, :, pl.ds(pl.multiple_of(m * 128, 128), 128)]
            part = tn(cols, left[s])[:ROWS]
            acc[m] = part if first else acc[m] + part
            return carry

        lax.fori_loop(0, 8, one, 0)

    def send_back(q):
        for y_ in range(2):
            at = pl.multiple_of(q * 16, 16)
            rows = acc[:, pl.ds(at, 16), :][:, y_ * 8 : y_ * 8 + 8, :].reshape(64, 1024).astype(BF16)
            for t_ in range(8):
                osend[q, y_ * 8 + t_] = rows[:, t_ * 128 : t_ * 128 + 128]

        def one(d, carry):
            t_, y_ = lax.rem(t + d // 2, 8), lax.rem(y + lax.rem(d, 2), 2)
            pltpu.make_async_remote_copy(
                src_ref=osend.at[q, y_ * 8 + t_], dst_ref=oback.at[q, h, b], send_sem=os_.at[q], recv_sem=or_.at[q],
                device_id=(a * 8 + t_, z * 2 + y_), device_id_type=MESH,
            ).start()
            return carry

        lax.fori_loop(1, 16, one, 0)
        pltpu.make_async_copy(osend.at[q, y * 8 + t], oback.at[q, h, b], or_.at[q]).start()

    def view(buffer, g, plane):
        return buffer.at[g, plane] if g < 2 else buffer.at[g, plane, :, pl.ds(0, SHORT_PAD)]

    def fold_chunks(g):
        for q in (2 * g, 2 * g + 1) if g < 2 else (4,):
            pltpu.make_async_copy(oback.at[q], oback.at[q], or_.at[q]).wait()

        def pieces(q, b_, m2, e):
            fbuf[...] = oback[q, :, b_, pl.ds(pl.multiple_of(m2 * 16, 16), 16), :].astype(F32)
            return [fbuf[:, e * STEP + k, :] for k in range(STEP)]

        def two_planes(n, carry):
            b_, m2 = n // 4, lax.rem(n, 4)
            for e in range(2):
                plane = (2 * m2 + e) * 2 + b_
                if g < 2:
                    rows = [fold(pieces(2 * g + f, b_, m2, e)) for f in range(2)]
                    fold_send[g, plane] = jnp.concatenate(rows, axis=0).astype(BF16)
                else:
                    whole = pieces(4, b_, m2, e)
                    rows = [fold(whole[:4]), fold(whole[4:])]
                    fold_send[g, plane, :, :SHORT_PAD] = jnp.concatenate(rows, axis=0).astype(BF16)
            return carry

        lax.fori_loop(0, 8, two_planes, 0)
        pltpu.make_async_copy(view(fold_send, g, z), view(fold_got, g, z), fr.at[g]).start()

        def one(d, carry):
            there = lax.rem(z + d, PLANES)
            pltpu.make_async_remote_copy(
                src_ref=view(fold_send, g, there), dst_ref=view(fold_got, g, z), send_sem=fs.at[g], recv_sem=fr.at[g],
                device_id=at_plane(there), device_id_type=MESH,
            ).start()
            return carry

        lax.fori_loop(1, PLANES, one, 0)

    def project(x):
        centered = x - jnp.mean(x, axis=0, keepdims=True)
        variance = jnp.mean(centered * centered, axis=0, keepdims=True)
        return tn((centered * lax.rsqrt(variance + EPS)).astype(BF16), wo_ref[...])

    def finish(g):
        arrived = fold_got.at[g] if g < 2 else fold_got.at[g, :, :, pl.ds(0, SHORT_PAD)]
        pltpu.make_async_copy(arrived, arrived, fr.at[g]).wait()
        if g < 2:
            x = fold_got[g].astype(F32)
            for f in range(2):
                part = project(x[:, f * 8 : f * 8 + 8, :].reshape(CH, WIDE))
                lin[f] = (part * gate[2 * g + f]).reshape(STEP, ROWS, CH)
        else:
            x = fold_got[g, :, :, :SHORT_PAD].astype(F32)
            for f in range(2):
                part = project(x[:, f * 8 : f * 8 + 8, :].reshape(CH, SHORT_PAD))[:SHORT]
                lin[0, f * 4 : f * 4 + 4] = (part * gate[4, f * SHORT : f * SHORT + SHORT]).reshape(4, ROWS, CH)

        def eight_rows(n, carry):
            at = pl.multiple_of(lax.rem(n, 5) * 16 + (n // 5) * 8, 8)
            rows = pl.ds(pl.multiple_of(n * 8, 8), 8)
            if g < 2:
                both = [jnp.swapaxes(lin[f, :, pl.ds(at, 8), :], 0, 1) for f in range(2)]
                out_ref[rows, g * 16 : g * 16 + 16, :] = jnp.concatenate(both, axis=1).astype(BF16)
            else:
                out_ref[rows, 32:40, :] = jnp.swapaxes(lin[0, :, pl.ds(at, 8), :], 0, 1).astype(BF16)
            return carry

        lax.fori_loop(0, 10, eight_rows, 0)

    for s in range(CHUNKS):
        normalise(s)
        factors(s)
        if s == 0:
            pl.semaphore_wait(barrier, 46)
        send_planes(s)

    def gates(s, carry):
        gate[s] = jax.nn.sigmoid(jnp.dot(normed[s], wog_ref[...], preferred_element_type=F32))
        return carry

    lax.fori_loop(0, CHUNKS, gates, 0)

    for s in range(CHUNKS):
        pltpu.make_async_copy(got.at[s], got.at[s], zr.at[s]).wait()
        unfold_chunk(s)
        send_inside(s)
        if s:
            multiply(s - 1, s == 1)
    multiply(CHUNKS - 1, False)
    for q in range(CHUNKS):
        send_back(q)
    for g in range(3):
        fold_chunks(g)
    for g in range(3):
        finish(g)

    for s in range(CHUNKS):
        sent = got.at[s, pl.ds(0, PLANES - 1)]
        pltpu.make_async_copy(sent, sent, zs.at[s]).wait()
        sent = tiles.at[s, pl.ds(0, 15)]
        pltpu.make_async_copy(sent, sent, pls.at[s]).wait()
        pltpu.make_async_copy(sent, sent, prs.at[s]).wait()
        sent = osend.at[s, pl.ds(0, 15)]
        pltpu.make_async_copy(sent, sent, os_.at[s]).wait()
    for g in range(3):
        sent = fold_got.at[g, pl.ds(0, PLANES - 1)] if g < 2 else fold_got.at[g, pl.ds(0, PLANES - 1), :, pl.ds(0, SHORT_PAD)]
        pltpu.make_async_copy(sent, sent, fs.at[g]).wait()


def on_device(*args):
    vmem = pltpu.VMEM
    return pl.pallas_call(
        kernel,
        out_shape=jax.ShapeDtypeStruct((ROWS, COLS, CH), BF16),
        in_specs=[pl.BlockSpec(memory_space=vmem)] * 7,
        out_specs=pl.BlockSpec(memory_space=vmem),
        scratch_shapes=[
            vmem((ROWS, COLS, CH), F32),
            vmem((4, CH, CH), BF16),
            vmem((STEP, ROWS, CH), F32),
            vmem((CHUNKS, WIDE, CH), BF16),
            vmem((CHUNKS, WIDE, CH), F32),
            vmem((CHUNKS, PLANES, 16, WIDE), BF16),
            vmem((CHUNKS, PLANES, 16, WIDE), BF16),
            vmem((16, 16, CH), F32),
            vmem((CHUNKS, 16, 128, 128), BF16),
            vmem((CHUNKS, 256, 1024), BF16),
            vmem((CHUNKS, 256, 1024), BF16),
            vmem((8, ROWS, 1024), F32),
            vmem((CHUNKS, 16, 64, 128), BF16),
            vmem((CHUNKS, 8, 2, 64, 128), BF16),
            vmem((8, 16, CH), F32),
            vmem((3, PLANES, 16, WIDE), BF16),
            vmem((3, PLANES, 16, WIDE), BF16),
            vmem((2, STEP, ROWS, CH), F32),
        ]
        + [pltpu.SemaphoreType.DMA((CHUNKS,))] * 8
        + [pltpu.SemaphoreType.DMA((3,))] * 2,
        compiler_params=pltpu.CompilerParams(collective_id=0, has_side_effects=True, vmem_limit_bytes=48 * 2**20),
        cost_estimate=pl.CostEstimate(flops=2_000_000_000, bytes_accessed=4_000_000, transcendentals=2_000_000),
    )(*args)


def solution(mesh):
    in_specs = (P("row", "chan", None), P(), P(), P(), P(), P(), P())
    return jax.shard_map(
        on_device, mesh=mesh, in_specs=in_specs, out_specs=P("row", "chan", None), check_vma=False
    )
```

time: 301 us -> 168 us (0.56)
  Pallas kernels: 0 us -> 159 us
  blocking collectives: 154 us -> 0 us
  waiting for transfers between devices: 77.8 us -> 0 us
  matrix products: 15.2 us -> 0 us
  starting transfers between devices: 14.8 us -> 0 us
  between operations: 13.6 us -> 0.02 us
  local copies, waits for them, and re-layouts: 17.4 us -> 6.58 us
  other arithmetic: 7.33 us -> 0 us
    pallas_call x0 -> x1, Pallas kernels: none -> 159 us  [on_device(): pl.pallas_call(kernel, out_shape=jax.ShapeDtypeStruct((ROWS, COLS, CH), B...]
    all_to_all x2 -> x0, blocking collectives: 154 us -> none  [the longest x1 83.7 us: on_device(): lax.all_to_all(right_local, 'chan', split_axis=0, concat_axis=2, tiled=True)]
    all_to_all x1 -> x0, waiting for transfers between devices: 62.6 us -> none  [on_device(): lax.all_to_all(combined_slab, 'chan', split_axis=2, concat_axis=0, tiled=...]
    all_gather x1 -> x0, waiting for transfers between devices: 15.3 us -> none  [on_device(): right_all = lax.all_gather(right_slab, 'row', axis=1, tiled=True)]
    dot_general x7 -> x0, matrix products: 15.2 us -> none  [the longest x1 8.81 us: on_device(): jnp.einsum('hik,hjk->hij', left_slab, right_all, preferred_element_type=j...]
    all_to_all x1 -> x0, starting transfers between devices: 14.8 us -> none  [on_device(): lax.all_to_all(combined_slab, 'chan', split_axis=2, concat_axis=0, tiled=...]
    convert_element_type x3 -> x0, local copies, waits for them, and re-layouts: 12.1 us -> none  [the longest x2 9.9 us: on_device(): combined.astype(jnp.float32)]
    unnamed x14 -> x15, local copies, waits for them, and re-layouts: 0.36 us -> 6.58 us
  transfers between devices with their start and end apart: 2 -> 0, of which waited for: 2 -> 0; matrix products, arithmetic and copies ran while one was open for 1% -> 0% of each run, Pallas kernels for 0% -> 0%
where the time goes in v1:
time: 168 us; the launch traced here: 166 us
  Pallas kernels  159 us (95%)
  local copies, waits for them, and re-layouts  6.58 us (4%)
    pallas_call x1, Pallas kernels, on_device(): pl.pallas_call(kernel, out_shape=jax.ShapeDtypeStruct((ROWS, COLS, CH), B...  159 us
    unnamed x15, local copies, waits for them, and re-layouts  6.58 us

profile of v1, /device:TPU:1, one launch (start us, length us, event | category | flops | bytes accessed | tf_op | source)
XLA Modules:
  0.0 165.7 jit_solution(12721031695817063558)
XLA Ops:
  0.0 0.0 copy-start
  0.0 1.1 copy-done
  1.1 0.0 copy-start.1
  1.1 0.8 copy-done.1
  1.9 0.0 copy-start.2
  1.9 0.8 copy-done.2
  2.7 0.0 copy-start.3
  2.7 0.8 copy-done.3
  3.4 0.0 copy-start.4
  3.4 0.8 copy-done.4
  4.2 0.0 copy-start.5
  4.2 0.8 copy-done.5
  4.9 0.0 copy-start.6
  4.9 0.8 copy-done.6
  5.7 159.1 %shard_map.73 = bf16[80,40,128]{2,1,0:T(8,128)(2,1)S(1)} custom-call(bf16[80,40,128]{2,1,0:T(8,128)(2,1)S(1)} %copy-done, bf16[128,128]{1,0:T(8,128)(2,1)S(1)} %copy-done.1, bf16[128,128]{1,0:T(8,128)(2,1)S(1)} %copy-done.2, bf16[128,128]{1,0:T(8,128)(2,1)S(1)} %copy-done.3, bf16[128,128]{1,0:T(8,128)(2,1)S(1)} %copy-done.4, bf16[128,128]{1,0:T(8,128)(2,1)S(1)} %copy-done.5, ...), custom_call_target="tpu_custom_call" | custom-call | flops 2000000000 | bytes 4000000 | tf_op jit(solution)/shard_map/pallas_call | solution.py:292
  164.8 0.9 copy.9
Async XLA Ops:
  0.0 1.1 copy-start
  1.1 0.8 copy-start.1
  1.9 0.8 copy-start.2
  2.7 0.8 copy-start.3
  3.4 0.8 copy-start.4
  4.2 0.8 copy-start.5
  4.9 0.8 copy-start.6

commit v2 on v0

v2 whole, which is shorter than its diff:
```python
import functools

import jax
import jax.numpy as jnp
from jax import lax
from jax.experimental import pallas as pl
from jax.experimental.pallas import tpu as pltpu
from jax.sharding import PartitionSpec as P

MESH = pl.DeviceIdType.MESH
F32, BF16 = jnp.float32, jnp.bfloat16
EPS = 1e-05
ROWS, COLS, CH = 80, 40, 128
PLANES, CHUNKS, STEP = 16, 5, 8
WIDE = STEP * ROWS
SHORT, SHORT_PAD = WIDE // 2, 384
CUT, REST = 384, 256
MOVES = [(0, 0, WIDE), (1, 0, WIDE), (2, 0, WIDE), (3, 0, WIDE), (4, 0, CUT), (4, CUT, REST)]
BACK = (2 * CUT, 2 * REST + SHORT_PAD)


def nt(a, b):
    return lax.dot_general(a, b, (((1,), (1,)), ((), ())), preferred_element_type=F32)


def tn(a, b):
    return lax.dot_general(a, b, (((0,), (0,)), ((), ())), preferred_element_type=F32)


def unfold(x, k):
    start = k * ROWS
    tile, off = start // 128, start % 128
    lo = x[:, tile * 128 : tile * 128 + 128]
    if off == 0:
        return lo
    lo = pltpu.roll(lo, 128 - off, 1)
    if off + ROWS <= 128:
        return lo
    hi = pltpu.roll(x[:, tile * 128 + 128 : tile * 128 + 256], 128 - off, 1)
    lane = lax.broadcasted_iota(jnp.int32, lo.shape, 1)
    return jnp.where(lane < 128 - off, lo, hi)


def fold(pieces, first, last):
    tiles = {}
    lane = lax.broadcasted_iota(jnp.int32, pieces[0].shape, 1)
    for k, piece in enumerate(pieces):
        tile, off = k * ROWS // 128, k * ROWS % 128
        turned = pltpu.roll(piece, off, 1) if off else piece
        tiles[tile] = jnp.where(lane < off, tiles[tile], turned) if tile in tiles else turned
        if off + ROWS > 128:
            tiles[tile + 1] = turned
    return jnp.concatenate([tiles[tile] for tile in range(first, last)], axis=1)


def mix_halves(first, second):
    low = lax.broadcasted_iota(jnp.int32, first.shape, 1) < 4
    return jnp.where(low, first, pltpu.roll(second, 4, 1)), jnp.where(low, pltpu.roll(first, 4, 1), second)


def kernel(
    pair_hbm, wlg_hbm, wl_hbm, wrg_hbm, wr_hbm, wog_hbm, wo_hbm, out_ref,
    pair_ref, weights, pair32, wt, ns, normed, gate, send, got, flip, tiles, left, right, lk, rk, acc,
    osend, oback, flip4, fsend, fsend4, fgot, fgot4, lin,
    ins, zs, zr, pls, prs, plr, prr, os_, or_, fs, fr,
):
    r, c = lax.axis_index("row"), lax.axis_index("chan")
    z, y = c // 2, lax.rem(c, 2)
    a, t, core = r // 8, lax.rem(r, 8), lax.rem(r, 2)
    b = lax.rem(r // 4, 2)
    m = a * 4 + lax.rem(r, 4)
    h = lax.rem(r // 2, 2) * 2 + y

    def owner(g, h_, a_, b_):
        return ((2 * a_ + b_) * 4 + (h_ // 2) * 2 + g, z * 2 + lax.rem(h_, 2))

    def at_plane(z_):
        return (r, z_ * 2 + y)

    loads = [pltpu.make_async_copy(pair_hbm, pair_ref, ins.at[0])]
    for n, ref in enumerate((wlg_hbm, wl_hbm, wrg_hbm, wr_hbm, wog_hbm, wo_hbm)):
        loads.append(pltpu.make_async_copy(ref, weights.at[n], ins.at[n + 1]))
    for load in loads:
        load.start()

    barrier = pltpu.get_barrier_semaphore()

    def greet_plane(d, carry):
        pl.semaphore_signal(barrier, inc=1, device_id=at_plane(lax.rem(z + d, PLANES)), device_id_type=MESH)
        return carry

    def greet_side(d, carry):
        there = (a * 8 + lax.rem(t + d // 2, 8), z * 2 + lax.rem(y + lax.rem(d, 2), 2))
        pl.semaphore_signal(barrier, inc=1, device_id=there, device_id_type=MESH)
        return carry

    def greet_across(d, carry):
        there = ((2 * (1 - a) + b) * 4 + d // 2, z * 2 + lax.rem(d, 2))
        pl.semaphore_signal(barrier, inc=1, device_id=there, device_id_type=MESH)
        return carry

    lax.fori_loop(1, PLANES, greet_plane, 0)
    lax.fori_loop(1, 16, greet_side, 0)
    lax.fori_loop(0, 8, greet_across, 0)

    for load in loads:
        load.wait()
    for n in range(2):
        lt = weights[n].astype(F32).T.reshape(PLANES, 8, CH)
        rt = weights[n + 2].astype(F32).T.reshape(PLANES, 8, CH)
        wt[n] = jnp.concatenate(mix_halves(lt, rt), axis=1).reshape(256, CH).astype(BF16)
    pair32[...] = pair_ref[...].astype(F32)

    def normalise(s):
        def eight_rows(g, carry):
            x = pair32[pl.ds(pl.multiple_of(g * 8, 8), 8), pl.ds(pl.multiple_of(s * STEP, STEP), STEP), :]
            centered = x - jnp.mean(x, axis=-1, keepdims=True)
            variance = jnp.mean(centered * centered, axis=-1, keepdims=True)
            at = pl.multiple_of(lax.rem(g, 5) * 16 + (g // 5) * 8, 8)
            ns[:, pl.ds(at, 8), :] = jnp.swapaxes(centered * lax.rsqrt(variance + EPS), 0, 1)
            return carry

        lax.fori_loop(0, 10, eight_rows, 0)
        normed[s] = ns[...].reshape(WIDE, CH).astype(BF16)

    def factors(s, w):
        n = normed[s]
        rows = pl.ds(pl.multiple_of(w * 64, 64), 64)
        return (jax.nn.sigmoid(nt(wt[0, rows, :], n)) * nt(wt[1, rows, :], n)).reshape(4, 16, WIDE)

    def send_planes(v):
        s, lanes = MOVES[v][0], pl.ds(MOVES[v][1], MOVES[v][2])
        to = got.at[s, z, :, lanes]
        pltpu.make_async_copy(send.at[s, z, :, lanes], to, zr.at[v]).start()

        def one(d, carry):
            there = lax.rem(z + d, PLANES)
            pltpu.make_async_remote_copy(
                src_ref=send.at[s, there, :, lanes], dst_ref=to, send_sem=zs.at[v], recv_sem=zr.at[v],
                device_id=at_plane(there), device_id_type=MESH,
            ).start()
            return carry

        lax.fori_loop(1, PLANES, one, 0)

    def single(w, carry):
        send[0, pl.ds(w * 4, 4)] = factors(4, w).astype(BF16)
        return carry

    def double(p):
        def one(w, carry):
            v, u = factors(2 * p, w), factors(2 * p + 1, w)
            send[1 + p, pl.ds(w * 4, 4)] = jnp.concatenate([v[:, :8], u[:, :8]], axis=1).astype(BF16)
            send[3 + p, pl.ds(w * 4, 4)] = jnp.concatenate([v[:, 8:], u[:, 8:]], axis=1).astype(BF16)
            return carry

        lax.fori_loop(0, 4, one, 0)

    def arrive(v):
        arrived = got.at[MOVES[v][0], :, :, pl.ds(MOVES[v][1], MOVES[v][2])]
        pltpu.make_async_copy(arrived, arrived, zr.at[v]).wait()

    def turn(v):
        s, at, wide = MOVES[v]

        def one(z_, carry):
            flip[:, z_, at : at + wide] = got[s, z_, :, at : at + wide].astype(F32)
            return carry

        lax.fori_loop(0, PLANES, one, 0)
        tiles[s, :, :, :, at : at + wide] = flip[:, :, at : at + wide].reshape(2, 8, PLANES, wide).astype(BF16)

    def send_inside(v):
        s, lanes = MOVES[v][0], pl.ds(MOVES[v][1], MOVES[v][2])
        for g in range(2) if s == 0 else ((s - 1) // 2,):
            at = 0 if s == 0 else pl.ds(1 + 2 * ((s - 1) % 2), 2)
            n = 0 if s == 0 else 3 if v == 5 else 1 + (s - 1) % 2
            to_left, to_right = left.at[at, t, y, :, lanes], right.at[at, m, y, :, lanes]
            kk = g if s == 0 else pl.ds(0, 2)

            def from_left(h_, kk=kk):
                return tiles.at[s, kk, h_, :, lanes]

            def from_right(h_, kk=kk):
                return tiles.at[s, kk, 4 + h_, :, lanes]

            def to_owners(d, e, g=g, n=n, to_left=to_left, to_right=to_right, from_left=from_left, from_right=from_right):
                there = lax.rem(h + d, 4)
                pltpu.make_async_remote_copy(
                    src_ref=from_left(there), dst_ref=to_left, send_sem=pls.at[v], recv_sem=plr.at[n],
                    device_id=owner(g, there, a, lax.rem(b + e, 2)), device_id_type=MESH,
                ).start()
                pltpu.make_async_remote_copy(
                    src_ref=from_right(there), dst_ref=to_right, send_sem=prs.at[v], recv_sem=prr.at[n],
                    device_id=owner(g, there, lax.rem(a + e, 2), b), device_id_type=MESH,
                ).start()

            for e in range(2):

                def one(d, carry, e=e, to_owners=to_owners):
                    to_owners(d, e)
                    return carry

                lax.fori_loop(1 - e, 4, one, 0)

            @pl.when(core == g)
            def _(n=n, to_left=to_left, to_right=to_right, from_left=from_left, from_right=from_right):
                pltpu.make_async_copy(from_left(h), to_left, plr.at[n]).start()
                pltpu.make_async_copy(from_right(h), to_right, prr.at[n]).start()

            @pl.when(core != g)
            def _(to_owners=to_owners):
                to_owners(0, 0)

    def expect(n, at, lanes):
        for buffer, sem in ((left, plr), (right, prr)):
            arrived = buffer.at[at, :, :, :, lanes]
            pltpu.make_async_copy(arrived, arrived, sem.at[n]).wait()

    def multiply(chunks, columns, first=False):
        def unfold_block(i, carry):
            lanes = pl.ds(pl.multiple_of(i * 128, 128), 128)
            for n, (chunk, y_) in enumerate((chunk, y_) for chunk in chunks for y_ in range(2)):
                high = len(columns) * PLANES
                for source, target in ((left, lk), (right, rk)):
                    x = source[chunk, i, y_, :, : CUT if max(columns) < 4 else WIDE].astype(F32)
                    cols = [unfold(x, k) for k in columns]
                    target[n * high : n * high + high, lanes] = jnp.concatenate(cols, axis=0).astype(BF16)
            return carry

        lax.fori_loop(0, 8, unfold_block, 0)
        part = tn(rk[...], lk[...]).reshape(8, 128, 1024)[:, :ROWS]
        acc[...] = part if first else acc[...] + part

    def multiply_pair(n, split=False):
        pair = pl.ds(2 * n - 1, 2)
        expect(n, pair, pl.ds(0, CUT if split else WIDE))
        multiply((2 * n - 1, 2 * n), range(4))
        if split:
            expect(3, pair, pl.ds(CUT, REST))
        multiply((2 * n - 1, 2 * n), range(4, 8))

    def send_back(g):
        def to(d, part, start):
            t_, y_ = lax.rem(t + d // 2, 8), lax.rem(y + lax.rem(d, 2), 2)
            i = y_ * 8 + t_
            lanes = pl.ds(part * BACK[0], BACK[part])
            here, there = osend.at[i, :, lanes], oback.at[g, h, b, :, lanes]
            if start == 0:
                pltpu.make_async_copy(here, there, or_.at[2 * g + part]).start()
            else:
                pltpu.make_async_remote_copy(
                    src_ref=here, dst_ref=there, send_sem=os_.at[part], recv_sem=or_.at[2 * g + part],
                    device_id=(a * 8 + t_, z * 2 + y_), device_id_type=MESH,
                ).start()

        def block(d, start):
            t_, y_ = lax.rem(t + d // 2, 8), lax.rem(y + lax.rem(d, 2), 2)
            i = y_ * 8 + t_
            lanes = pl.ds(pl.multiple_of(t_ * 128, 128), 128)

            def pieces(q):
                rows = acc[:, pl.ds(pl.multiple_of(q * 16 + y_ * 8, 8), 8), lanes]
                turned = jnp.swapaxes(rows, 0, 1)
                return [turned[k] for k in range(STEP)]

            for qp in range(2):
                both = jnp.concatenate([fold(pieces(2 * qp + f), 0, 5) for f in range(2)], axis=0).astype(BF16)
                osend[i, :, qp * CUT : qp * CUT + CUT] = both[:, :CUT]
                osend[i, :, 2 * CUT + qp * REST : 2 * CUT + qp * REST + REST] = both[:, CUT:]
            last = pieces(4)
            both = jnp.concatenate([fold(last[:4], 0, 3), fold(last[4:], 0, 3)], axis=0).astype(BF16)
            osend[i, :, 2 * CUT + 2 * REST :] = both
            to(d, 0, start)

        def one(d, carry):
            block(d, 1)
            return carry

        def rest(d, carry):
            to(d, 1, 1)
            return carry

        lax.fori_loop(1, 16, one, 0)
        block(0, 0)
        lax.fori_loop(1, 16, rest, 0)
        to(0, 1, 0)

    def plane_of(b_, m_):
        return (m_ // 4) * 8 + b_ * 4 + m_ % 4

    def turn_back(g, part):
        arrived = oback.at[g, :, :, :, pl.ds(part * BACK[0], BACK[part])]
        pltpu.make_async_copy(arrived, arrived, or_.at[2 * g + part]).wait()
        at, wide = ((0, CUT), (CUT, REST))[part]
        lanes = slice(at, at + wide)

        def one(h_, carry):
            for b_ in range(2):
                for q in range(4):
                    begin = part * 2 * CUT + (q // 2) * wide
                    x = oback[g, h_, b_, :, begin : begin + wide].astype(F32)
                    flip[b_ * 8 : b_ * 8 + 8, q * 4 + h_, lanes] = x[(q % 2) * 8 : (q % 2) * 8 + 8]
            return carry

        lax.fori_loop(0, 4, one, 0)
        for b_ in range(2):
            for m_ in range(8):
                fsend[g, plane_of(b_, m_), :, lanes] = flip[b_ * 8 + m_, :, lanes].astype(BF16)

    def turn_back4():
        def one(i, carry):
            g, h_ = i // 4, lax.rem(i, 4)
            for b_ in range(2):
                x = oback[g, h_, b_, :, 2 * CUT + 2 * REST :].astype(F32)
                for f in range(2):
                    flip4[b_ * 8 : b_ * 8 + 8, f * 8 + i, :] = x[f * 8 : f * 8 + 8]
            return carry

        lax.fori_loop(0, 8, one, 0)
        for b_ in range(2):
            for m_ in range(8):
                fsend4[plane_of(b_, m_)] = flip4[b_ * 8 + m_].astype(BF16)

    def final(v, plane_out, plane_in):
        if v == 4:
            return fsend4.at[plane_out], fgot4.at[plane_in]
        lanes = pl.ds((v % 2) * CUT, (CUT, REST)[v % 2])
        return fsend.at[v // 2, plane_out, :, lanes], fgot.at[v // 2, plane_in, :, lanes]

    def send_final(v):
        here, to = final(v, z, z)
        pltpu.make_async_copy(here, to, fr.at[v]).start()

        def one(d, carry):
            there = lax.rem(z + d, PLANES)
            pltpu.make_async_remote_copy(
                src_ref=final(v, there, z)[0], dst_ref=to, send_sem=fs.at[v], recv_sem=fr.at[v],
                device_id=at_plane(there), device_id_type=MESH,
            ).start()
            return carry

        lax.fori_loop(1, PLANES, one, 0)

    def wait_final(v, sem, planes):
        target = final(v, z, pl.ds(0, planes))[1]
        pltpu.make_async_copy(target, target, sem.at[v]).wait()

    def project(x):
        centered = x - jnp.mean(x, axis=0, keepdims=True)
        variance = jnp.mean(centered * centered, axis=0, keepdims=True)
        return tn((centered * lax.rsqrt(variance + EPS)).astype(BF16), weights[5])

    def finish(qp):
        if qp < 2:
            rows = slice(qp * 8, qp * 8 + 8)
            both = mix_halves(fgot[0, :, rows, :].astype(F32), fgot[1, :, rows, :].astype(F32))
            for f in range(2):
                part = project(both[f].reshape(CH, WIDE))
                lin[f] = (part * gate[2 * qp + f]).reshape(STEP, ROWS, CH)
        else:
            x = fgot4[...].astype(F32)
            for f in range(2):
                part = project(x[:, f * 8 : f * 8 + 8, :].reshape(CH, SHORT_PAD))[:SHORT]
                lin[0, f * 4 : f * 4 + 4] = (part * gate[4, f * SHORT : f * SHORT + SHORT]).reshape(4, ROWS, CH)

        def eight_rows(n, carry):
            at = pl.multiple_of(lax.rem(n, 5) * 16 + (n // 5) * 8, 8)
            rows = pl.ds(pl.multiple_of(n * 8, 8), 8)
            if qp < 2:
                both = [jnp.swapaxes(lin[f, :, pl.ds(at, 8), :], 0, 1) for f in range(2)]
                out_ref[rows, qp * 16 : qp * 16 + 16, :] = jnp.concatenate(both, axis=1).astype(BF16)
            else:
                out_ref[rows, 32:40, :] = jnp.swapaxes(lin[0, :, pl.ds(at, 8), :], 0, 1).astype(BF16)
            return carry

        lax.fori_loop(0, 10, eight_rows, 0)

    normalise(4)
    lax.fori_loop(0, 4, single, 0)
    pl.semaphore_wait(barrier, 38)
    send_planes(0)
    for p in range(2):
        normalise(2 * p)
        normalise(2 * p + 1)
        double(p)
        send_planes(1 + p)
    for v in range(3, 6):
        send_planes(v)

    def gates(s, carry):
        gate[s] = jax.nn.sigmoid(jnp.dot(normed[s], weights[4], preferred_element_type=F32))
        return carry

    lax.fori_loop(0, CHUNKS, gates, 0)

    for v in range(4):
        arrive(v)
        turn(v)
        send_inside(v)
        if v == 1:
            expect(0, 0, pl.ds(0, WIDE))
            multiply((0,), range(8), True)
        if v >= 2:

            @pl.when(core == 0)
            def _(v=v):
                multiply_pair(v - 1)
                if v == 3:
                    send_back(0)

    arrive(4)
    turn(4)
    send_inside(4)

    @pl.when(core == 1)
    def _():
        multiply_pair(1)

    arrive(5)
    turn(5)
    send_inside(5)
    for part in range(2):
        turn_back(0, part)
        send_final(part)

    @pl.when(core == 1)
    def _():
        multiply_pair(2, True)
        send_back(1)

    for part in range(2):
        turn_back(1, part)
        send_final(2 + part)
    turn_back4()
    send_final(4)
    for v in range(4):
        wait_final(v, fr, PLANES)
    finish(0)
    finish(1)
    wait_final(4, fr, PLANES)
    finish(2)

    for v in range(6):
        s, lanes = MOVES[v][0], pl.ds(MOVES[v][1], MOVES[v][2])
        sent = got.at[s, pl.ds(0, PLANES - 1), :, lanes]
        pltpu.make_async_copy(sent, sent, zs.at[v]).wait()
        for here in range(2):
            n = 15 if v == 0 else 14 if here else 16
            sent = got.at[s, pl.ds(0, n), :, lanes]

            def inside(v=v, sent=sent):
                pltpu.make_async_copy(sent, sent, pls.at[v]).wait()
                pltpu.make_async_copy(sent, sent, prs.at[v]).wait()

            if v == 0 and here:
                inside()
            elif v:
                pl.when((core == (s - 1) // 2) == (here == 1))(inside)

    for part in range(2):
        sent = osend.at[pl.ds(0, 15), :, pl.ds(part * BACK[0], BACK[part])]
        pltpu.make_async_copy(sent, sent, os_.at[part]).wait()
    for v in range(5):
        wait_final(v, fs, PLANES - 1)


def on_device(*args):
    vmem, dma = pltpu.VMEM, pltpu.SemaphoreType.DMA
    return pl.pallas_call(
        kernel,
        out_shape=jax.ShapeDtypeStruct((ROWS, COLS, CH), BF16),
        in_specs=[pl.BlockSpec(memory_space=pl.ANY)] * 7,
        out_specs=pl.BlockSpec(memory_space=vmem),
        scratch_shapes=[
            vmem((ROWS, COLS, CH), BF16),
            vmem((6, CH, CH), BF16),
            vmem((ROWS, COLS, CH), F32),
            vmem((2, 256, CH), BF16),
            vmem((STEP, ROWS, CH), F32),
            vmem((CHUNKS, WIDE, CH), BF16),
            vmem((CHUNKS, WIDE, CH), F32),
            vmem((CHUNKS, PLANES, 16, WIDE), BF16),
            vmem((CHUNKS, PLANES, 16, WIDE), BF16),
            vmem((16, 16, WIDE), F32),
            vmem((CHUNKS, 2, 8, PLANES, WIDE), BF16),
            vmem((CHUNKS, 8, 2, PLANES, WIDE), BF16),
            vmem((CHUNKS, 8, 2, PLANES, WIDE), BF16),
            vmem((256, 1024), BF16),
            vmem((256, 1024), BF16),
            vmem((8, ROWS, 1024), F32),
            vmem((16, 16, sum(BACK)), BF16),
            vmem((2, 4, 2, 16, sum(BACK)), BF16),
            vmem((16, 16, SHORT_PAD), F32),
            vmem((2, PLANES, 16, WIDE), BF16),
            vmem((PLANES, 16, SHORT_PAD), BF16),
            vmem((2, PLANES, 16, WIDE), BF16),
            vmem((PLANES, 16, SHORT_PAD), BF16),
            vmem((2, STEP, ROWS, CH), F32),
            dma((7,)),
        ]
        + [dma((6,))] * 4
        + [dma((4,))] * 2
        + [dma((2,)), dma((4,)), dma((5,)), dma((5,))],
        compiler_params=pltpu.CompilerParams(collective_id=0, has_side_effects=True, vmem_limit_bytes=60 * 2**20),
        cost_estimate=pl.CostEstimate(flops=2_000_000_000, bytes_accessed=4_000_000, transcendentals=2_000_000),
    )(*args)


def solution(mesh):
    in_specs = (P("row", "chan", None), P(), P(), P(), P(), P(), P())
    return jax.shard_map(
        on_device, mesh=mesh, in_specs=in_specs, out_specs=P("row", "chan", None), check_vma=False
    )
```

time: 301 us -> 140 us (0.47)
  blocking collectives: 154 us -> 0 us
  Pallas kernels: 0 us -> 138 us
  waiting for transfers between devices: 77.8 us -> 0 us
  local copies, waits for them, and re-layouts: 17.4 us -> 2.11 us
  matrix products: 15.2 us -> 0 us
  starting transfers between devices: 14.8 us -> 0 us
  between operations: 13.6 us -> 0.01 us
  other arithmetic: 7.33 us -> 0 us
    all_to_all x2 -> x0, blocking collectives: 154 us -> none  [the longest x1 83.7 us: on_device(): lax.all_to_all(right_local, 'chan', split_axis=0, concat_axis=2, tiled=True)]
    pallas_call x0 -> x1, Pallas kernels: none -> 138 us  [on_device(): pl.pallas_call(kernel, out_shape=jax.ShapeDtypeStruct((ROWS, COLS, CH), B...]
    all_to_all x1 -> x0, waiting for transfers between devices: 62.6 us -> none  [on_device(): lax.all_to_all(combined_slab, 'chan', split_axis=2, concat_axis=0, tiled=...]
    all_gather x1 -> x0, waiting for transfers between devices: 15.3 us -> none  [on_device(): right_all = lax.all_gather(right_slab, 'row', axis=1, tiled=True)]
    dot_general x7 -> x0, matrix products: 15.2 us -> none  [the longest x1 8.81 us: on_device(): jnp.einsum('hik,hjk->hij', left_slab, right_all, preferred_element_type=j...]
    all_to_all x1 -> x0, starting transfers between devices: 14.8 us -> none  [on_device(): lax.all_to_all(combined_slab, 'chan', split_axis=2, concat_axis=0, tiled=...]
    convert_element_type x3 -> x0, local copies, waits for them, and re-layouts: 12.1 us -> none  [the longest x2 9.9 us: on_device(): combined.astype(jnp.float32)]
    reduce_sum x4 -> x0, other arithmetic: 4.57 us -> none  [the longest x2 2.54 us: layer_norm(): variance = jnp.mean(centered * centered, axis=axis, keepdims=True)]
  transfers between devices with their start and end apart: 2 -> 0, of which waited for: 2 -> 0; matrix products, arithmetic and copies ran while one was open for 1% -> 0% of each run, Pallas kernels for 0% -> 0%
where the time goes in v2:
time: 140 us
  Pallas kernels  138 us (99%)
  local copies, waits for them, and re-layouts  2.11 us (2%)
    pallas_call x1, Pallas kernels, on_device(): pl.pallas_call(kernel, out_shape=jax.ShapeDtypeStruct((ROWS, COLS, CH), B...  138 us

profile of v2, /device:TPU:1, one launch (start us, length us, event | category | flops | bytes accessed | tf_op | source)
XLA Modules:
  0.0 139.7 jit_solution(8072839643835087221)
XLA Ops:
  0.0 137.6 %shard_map.73 = bf16[80,40,128]{2,1,0:T(8,128)(2,1)} custom-call(bf16[80,40,128]{2,1,0:T(8,128)(2,1)} %pair_hbm.1, bf16[128,128]{1,0:T(8,128)(2,1)} %wlg_hbm.1, bf16[128,128]{1,0:T(8,128)(2,1)} %wl_hbm.1, bf16[128,128]{1,0:T(8,128)(2,1)} %wrg_hbm.1, bf16[128,128]{1,0:T(8,128)(2,1)} %wr_hbm.1, bf16[128,128]{1,0:T(8,128)(2,1)} %wog_hbm.1, bf16[128,128]{1,0:T(8,128)(2,1)} %wo_hbm.1), custom_call_target="tpu_custom_call" | custom-call | flops 2000000000 | bytes 4000000 | tf_op jit(solution)/shard_map/pallas_call | solution.py:470
  137.6 2.1 %copy.9 = bf16[80,40,128]{2,1,0:T(8,128)(2,1)} copy(bf16[80,40,128]{2,1,0:T(8,128)(2,1)} %shard_map.73) | data formatting | bytes 1638400

commit v3 on v2

--- a/solution.py
+++ b/solution.py
@@ -15,7 +15,8 @@
 WIDE = STEP * ROWS
 SHORT, SHORT_PAD = WIDE // 2, 384
 CUT, REST = 384, 256
-MOVES = [(0, 0, WIDE), (1, 0, WIDE), (2, 0, WIDE), (3, 0, WIDE), (4, 0, CUT), (4, CUT, REST)]
+EARLY, LATE, EARLY_COLS = 512, 128, 6
+MOVES = [(0, 0, WIDE), (1, 0, WIDE), (2, 0, WIDE), (3, 0, WIDE), (4, 0, EARLY), (4, EARLY, LATE)]
 BACK = (2 * CUT, 2 * REST + SHORT_PAD)
 
 
@@ -67,12 +68,12 @@
     r, c = lax.axis_index("row"), lax.axis_index("chan")
     z, y = c // 2, lax.rem(c, 2)
     a, t, core = r // 8, lax.rem(r, 8), lax.rem(r, 2)
-    b = lax.rem(r // 4, 2)
+    b = lax.rem(r // 4 + a, 2)
     m = a * 4 + lax.rem(r, 4)
     h = lax.rem(r // 2, 2) * 2 + y
 
     def owner(g, h_, a_, b_):
-        return ((2 * a_ + b_) * 4 + (h_ // 2) * 2 + g, z * 2 + lax.rem(h_, 2))
+        return ((2 * a_ + lax.rem(a_ + b_, 2)) * 4 + (h_ // 2) * 2 + g, z * 2 + lax.rem(h_, 2))
 
     def at_plane(z_):
         return (r, z_ * 2 + y)
@@ -95,7 +96,7 @@
         return carry
 
     def greet_across(d, carry):
-        there = ((2 * (1 - a) + b) * 4 + d // 2, z * 2 + lax.rem(d, 2))
+        there = ((2 * (1 - a) + lax.rem(1 - a + b, 2)) * 4 + d // 2, z * 2 + lax.rem(d, 2))
         pl.semaphore_signal(barrier, inc=1, device_id=there, device_id_type=MESH)
         return carry
 
@@ -167,7 +168,11 @@
             flip[:, z_, at : at + wide] = got[s, z_, :, at : at + wide].astype(F32)
             return carry
 
-        lax.fori_loop(0, PLANES, one, 0)
+        if wide > LATE:
+            lax.fori_loop(0, PLANES, one, 0)
+        else:
+            for z_ in range(PLANES):
+                flip[:, z_, at : at + wide] = got[s, z_, :, at : at + wide].astype(F32)
         tiles[s, :, :, :, at : at + wide] = flip[:, :, at : at + wide].reshape(2, 8, PLANES, wide).astype(BF16)
 
     def send_inside(v):
@@ -223,22 +228,26 @@
             for n, (chunk, y_) in enumerate((chunk, y_) for chunk in chunks for y_ in range(2)):
                 high = len(columns) * PLANES
                 for source, target in ((left, lk), (right, rk)):
-                    x = source[chunk, i, y_, :, : CUT if max(columns) < 4 else WIDE].astype(F32)
+                    x = source[chunk, i, y_, :, : EARLY if max(columns) < EARLY_COLS else WIDE].astype(F32)
                     cols = [unfold(x, k) for k in columns]
                     target[n * high : n * high + high, lanes] = jnp.concatenate(cols, axis=0).astype(BF16)
             return carry
 
         lax.fori_loop(0, 8, unfold_block, 0)
-        part = tn(rk[...], lk[...]).reshape(8, 128, 1024)[:, :ROWS]
+        deep = len(chunks) * 2 * len(columns) * PLANES
+        part = tn(rk[:deep], lk[:deep]).reshape(8, 128, 1024)[:, :ROWS]
         acc[...] = part if first else acc[...] + part
 
-    def multiply_pair(n, split=False):
-        pair = pl.ds(2 * n - 1, 2)
-        expect(n, pair, pl.ds(0, CUT if split else WIDE))
+    def multiply_pair(n):
+        expect(n, pl.ds(2 * n - 1, 2), pl.ds(0, WIDE))
         multiply((2 * n - 1, 2 * n), range(4))
-        if split:
-            expect(3, pair, pl.ds(CUT, REST))
-        multiply((2 * n - 1, 2 * n), range(4, 8))
+        multiply((2 * n - 1, 2 * n), range(4, STEP))
+
+    def multiply_last():
+        expect(2, pl.ds(3, 2), pl.ds(0, EARLY))
+        multiply((3, 4), range(EARLY_COLS))
+        expect(3, pl.ds(3, 2), pl.ds(EARLY, LATE))
+        multiply((3, 4), range(EARLY_COLS, STEP))
 
     def send_back(g):
         def to(d, part, start):
@@ -287,7 +296,7 @@
         to(0, 1, 0)
 
     def plane_of(b_, m_):
-        return (m_ // 4) * 8 + b_ * 4 + m_ % 4
+        return (m_ // 4) * 8 + (b_ + m_ // 4) % 2 * 4 + m_ % 4
 
     def turn_back(g, part):
         arrived = oback.at[g, :, :, :, pl.ds(part * BACK[0], BACK[part])]
@@ -426,7 +435,7 @@
 
     @pl.when(core == 1)
     def _():
-        multiply_pair(2, True)
+        multiply_last()
         send_back(1)
 
     for part in range(2):
@@ -486,8 +495,8 @@
             vmem((CHUNKS, 2, 8, PLANES, WIDE), BF16),
             vmem((CHUNKS, 8, 2, PLANES, WIDE), BF16),
             vmem((CHUNKS, 8, 2, PLANES, WIDE), BF16),
-            vmem((256, 1024), BF16),
-            vmem((256, 1024), BF16),
+            vmem((384, 1024), BF16),
+            vmem((384, 1024), BF16),
             vmem((8, ROWS, 1024), F32),
             vmem((16, 16, sum(BACK)), BF16),
             vmem((2, 4, 2, 16, sum(BACK)), BF16),

time: 140 us -> 138 us (0.986)
  Pallas kernels: 138 us -> 135 us
    pallas_call x1, Pallas kernels: 138 us -> 135 us  [on_device(): pl.pallas_call(kernel, out_shape=jax.ShapeDtypeStruct((ROWS, COLS, CH), B...]
where the time goes in v3:
time: 138 us; the launch traced here: 137 us
  Pallas kernels  135 us (98%)
  local copies, waits for them, and re-layouts  2.11 us (2%)
    pallas_call x1, Pallas kernels, on_device(): pl.pallas_call(kernel, out_shape=jax.ShapeDtypeStruct((ROWS, COLS, CH), B...  135 us

profile of v3, /device:TPU:1, one launch (start us, length us, event | category | flops | bytes accessed | tf_op | source)
XLA Modules:
  0.0 137.4 jit_solution(14983422100772173832)
XLA Ops:
  0.0 135.3 %shard_map.73 = bf16[80,40,128]{2,1,0:T(8,128)(2,1)} custom-call(bf16[80,40,128]{2,1,0:T(8,128)(2,1)} %pair_hbm.1, bf16[128,128]{1,0:T(8,128)(2,1)} %wlg_hbm.1, bf16[128,128]{1,0:T(8,128)(2,1)} %wl_hbm.1, bf16[128,128]{1,0:T(8,128)(2,1)} %wrg_hbm.1, bf16[128,128]{1,0:T(8,128)(2,1)} %wr_hbm.1, bf16[128,128]{1,0:T(8,128)(2,1)} %wog_hbm.1, bf16[128,128]{1,0:T(8,128)(2,1)} %wo_hbm.1), custom_call_target="tpu_custom_call" | custom-call | flops 2000000000 | bytes 4000000 | tf_op jit(solution)/shard_map/pallas_call | solution.py:479
  135.3 2.1 %copy.9 = bf16[80,40,128]{2,1,0:T(8,128)(2,1)} copy(bf16[80,40,128]{2,1,0:T(8,128)(2,1)} %shard_map.73) | data formatting | bytes 1638400

commit v4 on v3

--- a/solution.py
+++ b/solution.py
@@ -14,7 +14,7 @@
 PLANES, CHUNKS, STEP = 16, 5, 8
 WIDE = STEP * ROWS
 SHORT, SHORT_PAD = WIDE // 2, 384
-CUT, REST = 384, 256
+CUT, REST = 256, 384
 EARLY, LATE, EARLY_COLS = 512, 128, 6
 MOVES = [(0, 0, WIDE), (1, 0, WIDE), (2, 0, WIDE), (3, 0, WIDE), (4, 0, EARLY), (4, EARLY, LATE)]
 BACK = (2 * CUT, 2 * REST + SHORT_PAD)

time: 138 us -> 139 us (level)
  no operation moved by 1% of the time
where the time goes in v4:
time: 139 us; the launch traced here: 138 us
  Pallas kernels  136 us (98%)
  local copies, waits for them, and re-layouts  2.11 us (2%)
    pallas_call x1, Pallas kernels, on_device(): pl.pallas_call(kernel, out_shape=jax.ShapeDtypeStruct((ROWS, COLS, CH), B...  136 us

profile of v4, /device:TPU:1, one launch (start us, length us, event | category | flops | bytes accessed | tf_op | source)
XLA Modules:
  0.0 138.4 jit_solution(5741949892333526662)
XLA Ops:
  0.0 136.3 %shard_map.73 = bf16[80,40,128]{2,1,0:T(8,128)(2,1)} custom-call(bf16[80,40,128]{2,1,0:T(8,128)(2,1)} %pair_hbm.1, bf16[128,128]{1,0:T(8,128)(2,1)} %wlg_hbm.1, bf16[128,128]{1,0:T(8,128)(2,1)} %wl_hbm.1, bf16[128,128]{1,0:T(8,128)(2,1)} %wrg_hbm.1, bf16[128,128]{1,0:T(8,128)(2,1)} %wr_hbm.1, bf16[128,128]{1,0:T(8,128)(2,1)} %wog_hbm.1, bf16[128,128]{1,0:T(8,128)(2,1)} %wo_hbm.1), custom_call_target="tpu_custom_call" | custom-call | flops 2000000000 | bytes 4000000 | tf_op jit(solution)/shard_map/pallas_call | solution.py:479
  136.3 2.1 %copy.9 = bf16[80,40,128]{2,1,0:T(8,128)(2,1)} copy(bf16[80,40,128]{2,1,0:T(8,128)(2,1)} %shard_map.73) | data formatting | bytes 1638400
